TPU v7x, 32 devices: a whole 2x2x4 slice. The times are simulated.
32 devices in a mesh: groups: 2 (over x), bl: 16 (over z, y, core).
Axes of the slice: x: 2, y: 2, z: 4, core: 2. Of those that a mesh axis runs over, the one named last changes fastest.
Arguments:
- grid: bfloat16 [32, 1024, 2048], P(('groups', 'bl')), parts along dimension 0, may hold values from -6 to 6
- patch_owner: int32 [4096, 1], P(('groups', 'bl')), parts along dimension 0, may hold values from 0 to 15; in each aligned block of 128 rows (0 to 127, 128 to 255, ...) at most 12 rows name the same one
- patch_column: int32 [4096], P(('groups', 'bl')), parts along dimension 0, may hold values from 0 to 1023
- aperture_index: int32 [4096], P(('groups', 'bl')), parts along dimension 0, may hold values from 0 to 7
- w_index: int32 [4096, 8], P(('groups', 'bl')), parts along dimension 0, may hold values from 0 to 31
- a_kernels: float32 [8, 2, 1024], replicated, may hold values from -6 to 6
- w_kernels: float32 [32, 2, 1024], replicated, may hold values from -6 to 6
- channel_response: bfloat16 [2, 1024, 128], P(None, None, 'groups'), parts along dimension 2, may hold values from -0.125 to 0.125
- time_owner: int32 [4096, 1], P(('groups', 'bl')), parts along dimension 0, may hold values from 0 to 15; in each aligned block of 128 rows (0 to 127, 128 to 255, ...) at most 12 rows name the same one
- observed: bfloat16 [6144, 1024], P(('groups', 'bl')), parts along dimension 0, may hold values from -6 to 6
Outputs:
- residual: bfloat16 [6144, 1024], P(('groups', 'bl')), parts along dimension 0
There are 2 independent parts, one for each index of `groups`. A program takes and returns all parts, laid end to end along the dimension named above; an argument that names none is the same for every part. Nothing has to cross between parts.
Inputs may be any that keep to these rules, and one draw needn't show every extreme that they name: `patch_owner`: within the rows of one device no owner is named by more than 12 rows, a bound that some block reaches. `time_owner`: within the rows of one device no owner is named by more than 12 rows, a bound that some block reaches.
All inputs are finite; a program needn't handle non-finite values.
Results may differ from a plain program's by a relative error of at most 0.0052.
Values may be sent and summed in bfloat16 or wider, within the bound.
A program may use at most 64 MiB of HBM per device.

v0:
```python
import jax
import jax.numpy as jnp
from jax import lax
from jax.sharding import PartitionSpec as P


def slot_of(owner_column, peer_count, capacity):
    owners = owner_column[:, 0]
    hits = (owners[:, None] == jnp.arange(peer_count, dtype=jnp.int32)[None, :]).astype(jnp.int32)
    before = jnp.cumsum(hits, axis=0) - hits
    ranks = jnp.sum(before * hits, axis=1)
    return owners * capacity + ranks


def response_matrix(channel_response):
    real_part = channel_response[0]
    imag_part = channel_response[1]
    upper_half = jnp.concatenate([real_part, imag_part], axis=1)
    lower_half = jnp.concatenate([-imag_part, real_part], axis=1)
    return jnp.concatenate([upper_half, lower_half], axis=0)


def predict(patches, aperture, wplanes, a_kernels, w_kernels, matrix):
    row_count = patches.shape[0]
    cells = patches.shape[1] // 2
    values = patches.astype(jnp.float32)
    patch_re = values[:, :cells]
    patch_im = values[:, cells:]
    a_chosen = jnp.take(a_kernels, aperture, axis=0)
    taper_re = patch_re * a_chosen[:, 0] - patch_im * a_chosen[:, 1]
    taper_im = patch_re * a_chosen[:, 1] + patch_im * a_chosen[:, 0]
    screen = jnp.take(w_kernels, wplanes, axis=0)
    weight_re = taper_re[:, None, :] * screen[:, :, 0] - taper_im[:, None, :] * screen[:, :, 1]
    weight_im = taper_re[:, None, :] * screen[:, :, 1] + taper_im[:, None, :] * screen[:, :, 0]
    weighted = jnp.concatenate([weight_re, weight_im], axis=2).astype(jnp.bfloat16)
    samples = wplanes.shape[1]
    product = jnp.dot(
        weighted.reshape(row_count * samples, -1), matrix, preferred_element_type=jnp.float32
    )
    return product.reshape(row_count, -1).astype(jnp.bfloat16)


def local(
    grid,
    patch_owner,
    patch_column,
    aperture_index,
    w_index,
    a_kernels,
    w_kernels,
    channel_response,
    time_owner,
    observed,
):
    peer_count = lax.axis_size("bl")
    capacity = observed.shape[0] // peer_count
    matrix = response_matrix(channel_response)
    grid_tiles = grid[0]
    patch_slots = slot_of(patch_owner, peer_count, capacity)
    requests = jnp.zeros((peer_count * capacity,), jnp.int32).at[patch_slots].set(patch_column)
    requests = requests.reshape(peer_count, capacity, 1)
    received = lax.all_to_all(requests, "bl", split_axis=0, concat_axis=0, tiled=True)
    senders = received.shape[0]
    item_count = received.shape[1]
    pieces = jnp.take(grid_tiles, received.reshape(-1), axis=0).reshape(senders, item_count, -1)
    answered = lax.all_to_all(pieces, "bl", split_axis=0, concat_axis=0, tiled=True)
    gathered = answered.reshape(peer_count * capacity, -1)[patch_slots]
    predicted = predict(gathered, aperture_index, w_index, a_kernels, w_kernels, matrix)
    targets = slot_of(time_owner, peer_count, capacity)
    outgoing = (
        jnp.zeros((peer_count * capacity, predicted.shape[1]), jnp.bfloat16)
        .at[targets]
        .set(predicted)
    )
    outgoing = outgoing.reshape(peer_count, capacity, -1)
    arrived = lax.all_to_all(outgoing, "bl", split_axis=0, concat_axis=0, tiled=True).reshape(
        peer_count * capacity, -1
    )
    return (observed.astype(jnp.float32) - arrived.astype(jnp.float32)).astype(jnp.bfloat16)


def solution(mesh):
    in_specs = (
        P(("groups", "bl"), None, None),
        P(("groups", "bl"), None),
        P(("groups", "bl")),
        P(("groups", "bl")),
        P(("groups", "bl"), None),
        P(),
        P(),
        P(None, None, "groups"),
        P(("groups", "bl"), None),
        P(("groups", "bl"), None),
    )
    out_specs = P(("groups", "bl"), None)
    return jax.shard_map(local, mesh=mesh, in_specs=in_specs, out_specs=out_specs, check_vma=False)
```

profile of v0, /device:TPU:0, one launch (start us, length us, event | category | flops | bytes accessed | tf_op | source)
XLA Modules:
  0.0 116.3 jit_solution(456857085700492443)
XLA Ops:
  0.0 0.8 fusion.20
  0.8 0.2 reduce_window_sum.18
  1.0 0.8 select_reduce_fusion
  1.8 0.7 fusion.23
  2.5 1.1 scatter_custom_fusion
  3.6 0.7 reshape.85
  4.3 7.4 %all-to-all-start = ((s32[16,12,1]{1,2,0:T(1,128)}), s32[16,12,1]{1,2,0:T(1,128)S(1)}, u32[]{:S(2)}, u32[]{:S(2)}) async-start(s32[16,12,1]{1,2,0:T(1,128)} %bitcast.6), calls=%async_computation | async-start | bytes 16384 | tf_op jit(solution)/shard_map/all_to_all | solution.py:62
  11.7 0.7 compare_select_fusion.1
  12.3 0.7 compare_and_fusion.1
  13.0 0.7 compare_select_fusion.3
  13.7 0.7 compare_and_fusion.2
  14.4 1.0 slice_bitcast_fusion.2
  15.3 0.9 fusion.27
  16.3 0.7 fusion.21
  17.0 0.2 reduce_window_sum.17
  17.2 1.4 %select_reduce_fusion.1 = s32[128]{0:T(128)} fusion(s32[128,16]{1,0:T(8,128)S(1)} %reduce_window_sum.17, s32[128]{0:T(128)} %bitcast.69), kind=kLoop, calls=%fused_computation.41 | loop fusion | flops 10112 | bytes 9216 | tf_op jit(solution)/shard_map/reduce_sum | solution.py:11
  18.5 0.1 copy.18
  18.6 0.1 reshape.117
  18.7 0.1 copy.17
  18.9 17.3 %gather_fusion.3 = f32[1024,2,1024]{2,1,0:T(2,128)} fusion(f32[32,2,1024]{2,1,0:T(2,128)S(1)} %copy-done, s32[1024]{0:T(1024)S(1)} %broadcast_clamp_fusion), kind=kCustom, calls=%fused_computation.3 | custom fusion | bytes 16781312 | tf_op jit(solution)/shard_map/jit(_take)/gather | solution.py:32
  36.2 8.5 %broadcast_select_fusion = f32[128,8,2,1024]{3,2,1,0:T(2,128)} fusion(f32[128,8,2,1024]{3,2,1,0:T(2,128)} %bitcast.62, pred[128,8]{1,0:T(8,128)(4,1)S(1)} %copy.17), kind=kLoop, calls=%fused_computation.6 | loop fusion | flops 2097152 | bytes 16778240 | tf_op jit(solution)/shard_map/jit(_take)/select_n | solution.py:32
  44.7 1.7 %gather_fusion.2 = f32[128,2,1024]{2,1,0:T(2,128)S(1)} fusion(f32[8,2,1024]{2,1,0:T(2,128)S(1)} %copy-done.1, s32[1024]{0:T(1024)S(1)} %pad_clamp_fusion), kind=kCustom, calls=%fused_computation.2 | custom fusion | bytes 2097664 | tf_op jit(solution)/shard_map/jit(_take)/gather | solution.py:29
  46.4 0.4 copy_select_fusion
  46.8 0.0 all-to-all-done
  46.8 0.5 broadcast.100
  47.4 0.7 reduce.3
  48.0 0.1 reshape.87
  48.1 4.6 %gather_fusion = bf16[192,2048]{1,0:T(8,128)(2,1)S(1)} fusion(bf16[1024,2048]{1,0:T(8,128)(2,1)} %bitcast.63, s32[1024]{0:T(1024)S(1)} %pad_clamp_fusion.2), kind=kCustom, calls=%fused_computation | custom fusion | bytes 1573632 | tf_op jit(solution)/shard_map/jit(_take)/gather | solution.py:65
  52.8 0.0 copy-start.4
  52.8 0.2 gather.18
  53.0 1.2 broadcast_select_fusion.1
  54.2 6.0 %all-to-all-start.1 = ((bf16[16,12,2048]{2,1,0:T(8,128)(2,1)}), bf16[16,12,2048]{2,1,0:T(8,128)(2,1)S(1)}, u32[]{:S(2)}, u32[]{:S(2)}) async-start(bf16[16,12,2048]{2,1,0:T(8,128)(2,1)} %broadcast_select_fusion.1), calls=%async_computation.1 | async-start | bytes 2097152 | tf_op jit(solution)/shard_map/all_to_all | solution.py:66
  60.2 11.8 %fusion.28 = (f32[128,8,1,1024]{3,2,1,0:T(1,128)}, f32[128,8,1,1024]{3,2,1,0:T(1,128)}) fusion(f32[128,8,2,1024]{3,2,1,0:T(2,128)} %broadcast_select_fusion), kind=kLoop, calls=%fused_computation.65 | loop fusion | bytes 16777216 | tf_op jit(solution)/shard_map/slice | solution.py:33
  72.0 11.1 %all-to-all-done.1 = bf16[16,12,2048]{2,1,0:T(8,128)(2,1)S(1)} async-done(((bf16[16,12,2048]{2,1,0:T(8,128)(2,1)}), bf16[16,12,2048]{2,1,0:T(8,128)(2,1)S(1)}, u32[]{:S(2)}, u32[]{:S(2)}) %all-to-all-start.1) | async-done | bytes 786464 | tf_op jit(solution)/shard_map/all_to_all | solution.py:66
  83.1 0.2 reshape.88
  83.3 0.9 gather_fusion.1
  84.2 0.1 convert_element_type.32
  84.4 0.2 multiply_subtract_fusion
  84.5 1.9 %copy-done.2 = f32[128,8,1,1024]{3,2,1,0:T(1,128)S(1)} copy-done((f32[128,8,1,1024]{3,2,1,0:T(1,128)S(1)}, f32[128,8,1,1024]{3,2,1,0:T(1,128)}, u32[]{:S(2)}) %copy-start.2) | copy-done | bytes 4194328
  86.4 5.0 %fusion.1 = (bf16[1024,1024]{1,0:T(8,128)(2,1)S(1)}, bf16[1024,1024]{1,0:T(8,128)(2,1)S(1)}) fusion(f32[128,8,1,1024]{3,2,1,0:T(1,128)} %get-tuple-element.8, f32[128,8,1,1024]{3,2,1,0:T(1,128)S(1)} %copy-done.2, f32[128,1024]{1,0:T(8,128)S(1)} %get-tuple-element.10, f32[128,1024]{1,0:T(8,128)S(1)} %get-tuple-element.9), kind=kLoop, calls=%fused_computation.12 | loop fusion | flops 8388608 | bytes 13631488 | tf_op jit(solution)/shard_map/convert.1
  91.5 1.3 %fusion.8 = bf16[1024,128]{1,0:T(8,128)(2,1)S(1)} fusion(bf16[1024,1024]{1,0:T(8,128)(2,1)S(1)} %get-tuple-element.6, bf16[1024,1024]{1,0:T(8,128)(2,1)S(1)} %get-tuple-element.5, bf16[1024,64]{0,1:T(8,128)(2,1)S(1)} %get-tuple-element.12, bf16[1024,64]{0,1:T(8,128)(2,1)S(1)} %fusion.27, bf16[1024,64]{0,1:T(8,128)(2,1)S(1)} %get-tuple-element.11), kind=kOutput, calls=%fused_computation.19 | convolution fusion | flops 547487744 | bytes 4849664 | tf_op jit(solution)/shard_map/dot_general | solution.py:37
  92.7 0.0 copy-start.3
  92.7 0.1 reshape.135
  92.9 1.3 %scatter_custom_fusion.1 = bf16[192,1024]{1,0:T(8,128)(2,1)S(1)} fusion(s32[128]{0:T(128)S(1)} %fusion.22, bf16[128,1024]{1,0:T(8,128)(2,1)S(1)} %reshape.135, bf16[]{:T(256)} %constant.36.clone.1), kind=kCustom, calls=%fused_computation.34 | custom fusion | bytes 393218 | tf_op jit(solution)/shard_map/scatter | solution.py:73
  94.1 0.1 reshape.89
  94.2 21.1 %all_to_all.15 = bf16[16,12,1024]{2,1,0:T(8,128)(2,1)S(1)} all-to-all(bf16[16,12,1024]{2,1,0:T(8,128)(2,1)S(1)} %reshape.89), channel_id=1, replica_groups=mesh['groups'=2,'bl'=16] {'bl'}, dimensions={0} | all-to-all | bytes 786432 | tf_op jit(solution)/shard_map/all_to_all | solution.py:76
  115.3 0.1 reshape.90
  115.4 0.8 subtract_convert_fusion
  (16 shorter events, 0.1 us)
Async XLA Ops:
  0.0 18.9 %copy-start = (f32[32,2,1024]{2,1,0:T(2,128)S(1)}, f32[32,2,1024]{2,1,0:T(2,128)}, u32[]{:S(2)}) copy-start(f32[32,2,1024]{2,1,0:T(2,128)} %param.16) | copy-start | bytes 786436
  4.3 42.6 %all-to-all-start = ((s32[16,12,1]{1,2,0:T(1,128)}), s32[16,12,1]{1,2,0:T(1,128)S(1)}, u32[]{:S(2)}, u32[]{:S(2)}) async-start(s32[16,12,1]{1,2,0:T(1,128)} %bitcast.6), calls=%async_computation | async-start | bytes 16384 | tf_op jit(solution)/shard_map/all_to_all | solution.py:62
  36.2 8.5 %copy-start.1 = (f32[8,2,1024]{2,1,0:T(2,128)S(1)}, f32[8,2,1024]{2,1,0:T(2,128)}, u32[]{:S(2)}) copy-start(f32[8,2,1024]{2,1,0:T(2,128)} %param.15) | copy-start | bytes 196612
  52.8 7.4 %copy-start.4 = (s32[128,1]{0,1:T(1,128)S(1)}, s32[128,1]{0,1:T(1,128)}, u32[]{:S(2)}) copy-start(s32[128,1]{0,1:T(1,128)} %param.18) | copy-start | bytes 1540
  53.0 7.2 %copy-start.5 = (s32[128]{0:T(128)S(1)}, s32[128]{0:T(128)}, u32[]{:S(2)}) copy-start(s32[128]{0:T(128)} %select_reduce_fusion.1) | copy-start | bytes 1540
  54.2 29.0 %all-to-all-start.1 = ((bf16[16,12,2048]{2,1,0:T(8,128)(2,1)}), bf16[16,12,2048]{2,1,0:T(8,128)(2,1)S(1)}, u32[]{:S(2)}, u32[]{:S(2)}) async-start(bf16[16,12,2048]{2,1,0:T(8,128)(2,1)} %broadcast_select_fusion.1), calls=%async_computation.1 | async-start | bytes 2097152 | tf_op jit(solution)/shard_map/all_to_all | solution.py:66
  84.2 2.2 %copy-start.2 = (f32[128,8,1,1024]{3,2,1,0:T(1,128)S(1)}, f32[128,8,1,1024]{3,2,1,0:T(1,128)}, u32[]{:S(2)}) copy-start(f32[128,8,1,1024]{3,2,1,0:T(1,128)} %get-tuple-element.7) | copy-start | bytes 12582916
  92.7 22.7 %copy-start.3 = (bf16[192,1024]{1,0:T(8,128)(2,1)S(1)}, bf16[192,1024]{1,0:T(8,128)(2,1)}, u32[]{:S(2)}) copy-start(bf16[192,1024]{1,0:T(8,128)(2,1)} %param.19) | copy-start | bytes 1179652
where the time goes:
time: 117 us; the launch traced here: 116 us
  local copies, waits for them, and re-layouts  43.8 us (37%)
  other arithmetic  25.3 us (22%)
  blocking collectives  21.1 us (18%)
  starting transfers between devices  13.4 us (11%)
  waiting for transfers between devices  11.1 us (9%)
  matrix products  1.25 us (1%)
    all_to_all x1, blocking collectives, local(): lax.all_to_all(outgoing, 'bl', split_axis=0, concat_axis=0, tiled=True)  21.1 us
    gather x1, local copies, waits for them, and re-layouts, predict(): screen = jnp.take(w_kernels, wplanes, axis=0)  17.3 us
    slice x1, local copies, waits for them, and re-layouts, predict(): screen[:, :, 0]  11.8 us
    all_to_all x1, waiting for transfers between devices, local(): lax.all_to_all(pieces, 'bl', split_axis=0, concat_axis=0, tiled=True)  11.1 us
    select_n x2, other arithmetic, predict(): screen = jnp.take(w_kernels, wplanes, axis=0)  9.23 us
    all_to_all x1, starting transfers between devices, local(): lax.all_to_all(requests, 'bl', split_axis=0, concat_axis=0, tiled=True)  7.39 us
    all_to_all x1, starting transfers between devices, local(): lax.all_to_all(pieces, 'bl', split_axis=0, concat_axis=0, tiled=True)  6.02 us
    another operation x1, other arithmetic  5.03 us
  transfers between devices with their start and end apart: 2, of which 1 were waited for; matrix products, arithmetic and copies ran while one was open for 40% of the time, Pallas kernels for 0%

commit v1 on v0

v1 whole, which is shorter than its diff:
```python
import functools

import jax
import jax.numpy as jnp
from jax import lax
from jax.experimental import pallas as pl
from jax.experimental.pallas import tpu as pltpu
from jax.sharding import PartitionSpec as P

F32 = jnp.float32
BF16 = jnp.bfloat16
LANES = 128


def iota(shape, axis):
    return lax.broadcasted_iota(jnp.int32, shape, axis)


def dot(a, b):
    return jnp.dot(a, b, preferred_element_type=F32)


def dot_nt(a, b):
    return lax.dot_general(a, b, (((1,), (1,)), ((), ())), preferred_element_type=F32)


def owner_and_rank(owner, n):
    rows = owner.shape[1]
    hits = (iota((n, rows), 0) == owner).astype(F32)
    earlier = (iota((rows, rows), 0) < iota((rows, rows), 1)).astype(F32).astype(BF16)
    before = dot(hits.astype(BF16), earlier)
    return owner, jnp.sum(before * hits, axis=0, keepdims=True).astype(jnp.int32)


def one_hot_rows(slot, count):
    return (iota((count, slot.shape[1]), 0) == slot).astype(F32).astype(BF16)


def kernel(
    n, cap, capp, ts, block,
    meta_ref, grid_hbm, a_ref, w_ref, chan_ref, obs_hbm,
    out_ref,
    grid, obs, rs, rq, acat, wcat, mat, tap, wt, sbuf, rbuf, wide, xbuf, sbuf2, rbuf2,
    local_sem, send_sem, req_sem, pred_sem, time_sem,
):
    me = lax.axis_index("bl")
    rows = meta_ref.shape[1]
    cells = grid.shape[1] // 2
    columns = grid.shape[0]
    span = cap * ts

    load_grid = pltpu.make_async_copy(grid_hbm, grid, local_sem.at[0])
    load_obs = pltpu.make_async_copy(obs_hbm, obs, local_sem.at[1])
    load_grid.start()
    load_obs.start()

    barrier = pltpu.get_barrier_semaphore()

    def greet(i, carry):
        pl.semaphore_signal(barrier, inc=1, device_id={"bl": lax.rem(me + i, n)},
                            device_id_type=pl.DeviceIdType.MESH)
        return carry

    lax.fori_loop(1, n, greet, 0)

    meta = meta_ref[...]
    p_owner, p_rank = owner_and_rank(meta[11:12], n)
    t_owner, t_rank = owner_and_rank(meta[12:13], n)
    data = jnp.concatenate([meta.astype(F32), jnp.zeros((LANES - 16, rows), F32)], axis=0).astype(BF16)
    wanted = dot_nt(one_hot_rows(p_owner * capp + p_rank, n * capp), data)
    rs[...] = wanted.reshape(n, capp, LANES)

    pl.semaphore_wait(barrier, n - 1)

    def request(i):
        peer = lax.rem(me + i, n)
        return pltpu.make_async_remote_copy(
            src_ref=rs.at[peer], dst_ref=rq.at[me], send_sem=send_sem.at[0, i], recv_sem=req_sem.at[me],
            device_id={"bl": peer}, device_id_type=pl.DeviceIdType.MESH)

    def predicted(i):
        peer = lax.rem(me + i, n)
        return pltpu.make_async_remote_copy(
            src_ref=sbuf.at[i - 1], dst_ref=rbuf.at[me], send_sem=send_sem.at[1, i], recv_sem=pred_sem.at[me],
            device_id={"bl": peer}, device_id_type=pl.DeviceIdType.MESH)

    def timed(i):
        peer = lax.rem(me + i, n)
        return pltpu.make_async_remote_copy(
            src_ref=sbuf2.at[peer], dst_ref=rbuf2.at[me], send_sem=send_sem.at[2, i], recv_sem=time_sem.at[me],
            device_id={"bl": peer}, device_id_type=pl.DeviceIdType.MESH)

    def arrival(buf, sem, i):
        sender = lax.rem(me + i, n)
        return pltpu.make_async_copy(buf.at[sender], buf.at[sender], sem.at[sender])

    def each(low, high, act):
        def step(i, carry):
            act(i)
            return carry
        lax.fori_loop(low, high, step, 0)

    each(1, n, lambda i: request(i).start())
    rq[me] = rs[me]

    for part in range(2):
        at = pl.ds(part * cells, cells)
        for source, table in ((a_ref, acat), (w_ref, wcat)):
            count = source.shape[0]
            value = source[:, part, :]
            high = value.astype(BF16)
            table[0:count, at] = high
            table[count:2 * count, at] = (value - high.astype(F32)).astype(BF16)
    ch = chan_ref.shape[2]
    left = (iota((ch, 2 * ch), 1) == iota((ch, 2 * ch), 0)).astype(F32).astype(BF16)
    right = (iota((ch, 2 * ch), 1) == iota((ch, 2 * ch), 0) + ch).astype(F32).astype(BF16)
    real, imag = chan_ref[0], chan_ref[1]
    mat[0:cells] = (dot(real, left) + dot(imag, right)).astype(BF16)
    mat[cells:2 * cells] = (dot(real, right) - dot(imag, left)).astype(BF16)
    move = dot_nt(one_hot_rows(t_owner * cap + t_rank, n * cap),
                  one_hot_rows(p_owner * cap + p_rank, n * cap)).astype(BF16)

    load_grid.wait()
    each(1, n, lambda i: arrival(rq, req_sem, i).wait())

    n_a = a_ref.shape[0]
    peers = min(n, 256 // capp)
    wide_step = 256

    def taper(b, carry):
        lot = peers * capp
        req = rq[pl.ds(b * peers, peers)].reshape(lot, LANES)
        column = req[:, 0:1] * 32.0 + req[:, 1:2]
        pick = (iota((lot, columns), 1).astype(F32) == column).astype(F32).astype(BF16)
        lane = iota((lot, 2 * n_a), 1)
        lane = jnp.where(lane >= n_a, lane - n_a, lane)
        a_pick = (lane.astype(F32) == req[:, 2:3]).astype(F32).astype(BF16)
        for start in range(0, cells, wide_step):
            re, im = pl.ds(start, wide_step), pl.ds(cells + start, wide_step)
            p_re, p_im = dot(pick, grid[:, re]), dot(pick, grid[:, im])
            a_re, a_im = dot(a_pick, acat[:, re]), dot(a_pick, acat[:, im])
            tap[pl.ds(b * peers, peers), :, re] = (p_re * a_re - p_im * a_im).reshape(peers, capp, wide_step)
            tap[pl.ds(b * peers, peers), :, im] = (p_re * a_im + p_im * a_re).reshape(peers, capp, wide_step)
        return carry

    lax.fori_loop(0, n // peers, taper, 0)

    n_w = w_ref.shape[0]

    def spread(value):
        return jnp.broadcast_to(value[:, None, :], (cap, ts, value.shape[1])).reshape(span, value.shape[1])

    def predict(c, carry):
        picks = []
        for j in range(block):
            req = spread(rq[lax.rem(me + c * block + j + 1, n), 0:cap, :])
            sample = iota((span, LANES), 0)
            mine = iota((span, LANES), 1) == 3 + jnp.bitwise_and(sample, ts - 1)
            plane = jnp.sum(jnp.where(mine, req, 0.0), axis=1, keepdims=True)
            lane = iota((span, 2 * n_w), 1)
            lane = jnp.where(lane >= n_w, lane - n_w, lane)
            picks.append((lane.astype(F32) == plane).astype(F32))
        w_pick = jnp.concatenate(picks, axis=0).astype(BF16)
        for start in range(0, cells, wide_step):
            re, im = pl.ds(start, wide_step), pl.ds(cells + start, wide_step)
            s_re, s_im = dot(w_pick, wcat[:, re]), dot(w_pick, wcat[:, im])
            for j in range(block):
                p = lax.rem(me + c * block + j + 1, n)
                t_re, t_im = spread(tap[p, 0:cap, re]), spread(tap[p, 0:cap, im])
                w_re, w_im = s_re[j * span:(j + 1) * span], s_im[j * span:(j + 1) * span]
                wt[pl.ds(j * span, span), re] = (t_re * w_re - t_im * w_im).astype(BF16)
                wt[pl.ds(j * span, span), im] = (t_re * w_im + t_im * w_re).astype(BF16)
        result = dot(wt[...], mat[...]).astype(BF16)
        sbuf[pl.ds(c * block, block)] = result.reshape(block, span, LANES)
        for j in range(block):
            i = c * block + j + 1

            @pl.when(i < n)
            def _():
                predicted(i).start()
        return carry

    lax.fori_loop(0, n // block, predict, 0)
    rbuf[me] = sbuf[n - 1]
    each(1, n, lambda i: arrival(rbuf, pred_sem, i).wait())

    total = n * cap
    wide[...] = rbuf[...].reshape(n * span, LANES).astype(F32)
    for t in range(ts):
        xbuf[:, pl.ds(t * LANES, LANES)] = wide[pl.ds(t, total, stride=ts), :].astype(BF16)
    moved = dot(move, xbuf[...])
    for t in range(ts):
        wide[pl.ds(t, total, stride=ts), :] = moved[:, t * LANES:(t + 1) * LANES]
    sbuf2[...] = wide[...].astype(BF16).reshape(n, span, LANES)
    each(1, n, lambda i: timed(i).start())
    rbuf2[me] = sbuf2[me]
    load_obs.wait()
    each(1, n, lambda i: arrival(rbuf2, time_sem, i).wait())

    wide[...] = rbuf2[...].reshape(n * span, LANES).astype(F32)
    for t in range(ts):
        at = pl.ds(t * LANES, LANES)
        out_ref[:, at] = (obs[:, at].astype(F32) - wide[pl.ds(t, total, stride=ts), :]).astype(BF16)

    def sent(i):
        request(i).wait_send()
        predicted(i).wait_send()
        timed(i).wait_send()

    each(1, n, sent)


def local(
    grid,
    patch_owner,
    patch_column,
    aperture_index,
    w_index,
    a_kernels,
    w_kernels,
    channel_response,
    time_owner,
    observed,
):
    n = lax.axis_size("bl")
    cap = observed.shape[0] // n
    capp = -(-cap // 8) * 8
    rows, ts = w_index.shape
    columns, width = grid.shape[1:]
    n_a, n_w = a_kernels.shape[0], w_kernels.shape[0]
    block = 4
    span = cap * ts
    meta = jnp.concatenate(
        [(patch_column >> 5)[None], (patch_column & 31)[None], aperture_index[None], w_index.T,
         patch_owner.T, time_owner.T, jnp.zeros((3, rows), jnp.int32)], axis=0)
    vmem = pl.BlockSpec(memory_space=pltpu.VMEM)
    hbm = pl.BlockSpec(memory_space=pl.ANY)
    return pl.pallas_call(
        functools.partial(kernel, n, cap, capp, ts, block),
        out_shape=jax.ShapeDtypeStruct(observed.shape, BF16),
        in_specs=[vmem, hbm, vmem, vmem, vmem, hbm],
        out_specs=vmem,
        scratch_shapes=[
            pltpu.VMEM((columns, width), BF16),
            pltpu.VMEM(observed.shape, BF16),
            pltpu.VMEM((n, capp, LANES), F32),
            pltpu.VMEM((n, capp, LANES), F32),
            pltpu.VMEM((2 * n_a, width), BF16),
            pltpu.VMEM((2 * n_w, width), BF16),
            pltpu.VMEM((width, 2 * channel_response.shape[2]), BF16),
            pltpu.VMEM((n, capp, width), F32),
            pltpu.VMEM((block * span, width), BF16),
            pltpu.VMEM((n, span, LANES), BF16),
            pltpu.VMEM((n, span, LANES), BF16),
            pltpu.VMEM((n * span, LANES), F32),
            pltpu.VMEM((n * cap, ts * LANES), BF16),
            pltpu.VMEM((n, span, LANES), BF16),
            pltpu.VMEM((n, span, LANES), BF16),
            pltpu.SemaphoreType.DMA((2,)),
            pltpu.SemaphoreType.DMA((3, n)),
            pltpu.SemaphoreType.DMA((n,)),
            pltpu.SemaphoreType.DMA((n,)),
            pltpu.SemaphoreType.DMA((n,)),
        ],
        compiler_params=pltpu.CompilerParams(
            collective_id=0, has_side_effects=True, vmem_limit_bytes=48 * 1024 * 1024),
    )(meta, grid.reshape(columns, width), a_kernels, w_kernels, channel_response, observed)


def solution(mesh):
    in_specs = (
        P(("groups", "bl"), None, None),
        P(("groups", "bl"), None),
        P(("groups", "bl")),
        P(("groups", "bl")),
        P(("groups", "bl"), None),
        P(),
        P(),
        P(None, None, "groups"),
        P(("groups", "bl"), None),
        P(("groups", "bl"), None),
    )
    out_specs = P(("groups", "bl"), None)
    return jax.shard_map(local, mesh=mesh, in_specs=in_specs, out_specs=out_specs, check_vma=False)
```

time: 117 us -> 45.2 us (0.39)
  the two profiles are of different devices: /device:TPU:0 before, /device:TPU:27 now
where the time goes in v1:
time: 45.2 us; the launch traced here: 44.9 us
  Pallas kernels  35.1 us (78%)
  local copies, waits for them, and re-layouts  9.08 us (20%)
  other arithmetic  0.66 us (1%)
    pallas_call x1, Pallas kernels, local(): pl.pallas_call(functools.partial(kernel, n, cap, capp, ts, block), out_sh...  35.1 us
    unnamed x10, local copies, waits for them, and re-layouts  6.94 us
    concatenate x1, local copies, waits for them, and re-layouts, local(): jnp.concatenate([(patch_column >> 5)[None], (patch_column & 31)[None], ap...  2.14 us

profile of v1, /device:TPU:27, one launch (start us, length us, event | category | flops | bytes accessed | tf_op | source)
XLA Modules:
  0.0 44.9 jit_solution(8676379752966869511)
XLA Ops:
  0.0 0.7 %and_bitcast_fusion = (s32[1,128]{1,0:T(1,128)S(1)}, s32[1,128]{1,0:T(1,128)S(1)}) fusion(s32[128]{0:T(128)} %param.12), kind=kLoop, calls=%fused_computation | loop fusion | flops 256 | bytes 1536 | tf_op jit(solution)/shard_map/broadcast_in_dim | solution.py:234
  0.7 2.1 %concatenate.3.meta_ref = s32[16,128]{1,0:T(8,128)S(1)} concatenate(s32[1,128]{1,0:T(1,128)S(1)} %get-tuple-element.6, s32[1,128]{1,0:T(1,128)S(1)} %get-tuple-element.5, s32[1,128]{1,0:T(1,128)} %bitcast.11, s32[8,128]{1,0:T(8,128)} %bitcast.10, s32[1,128]{1,0:T(1,128)} %bitcast.12, s32[1,128]{1,0:T(1,128)} %bitcast.13, s32[3,128]{1,0:T(4,128)S(1)} %broadcast_in_dim.15), dimensions={0} | concatenate | bytes 16384 | tf_op jit(solution)/shard_map/concatenate | solution.py:233
  2.8 1.2 %copy.11.chan_ref = bf16[2,1024,64]{2,1,0:T(8,128)(2,1)S(1)} copy(bf16[2,1024,64]{1,2,0:T(8,128)(2,1)} %param.17) | data formatting | bytes 524288 | tf_op args[7]
  4.0 0.0 copy-start
  4.0 2.2 %copy-done = bf16[1,1024,2048]{2,1,0:T(8,128)(2,1)S(1)} copy-done((bf16[1,1024,2048]{2,1,0:T(8,128)(2,1)S(1)}, bf16[1,1024,2048]{2,1,0:T(8,128)(2,1)}, u32[]{:S(2)}) %copy-start) | copy-done | bytes 4194328
  6.2 0.0 copy-start.1
  6.2 1.0 %copy-done.1 = bf16[192,1024]{1,0:T(8,128)(2,1)S(1)} copy-done((bf16[192,1024]{1,0:T(8,128)(2,1)S(1)}, bf16[192,1024]{1,0:T(8,128)(2,1)}, u32[]{:S(2)}) %copy-start.1) | copy-done | bytes 393240
  7.2 0.0 copy-start.2
  7.2 0.9 %copy-done.2 = f32[32,2,1024]{2,1,0:T(2,128)S(1)} copy-done((f32[32,2,1024]{2,1,0:T(2,128)S(1)}, f32[32,2,1024]{2,1,0:T(2,128)}, u32[]{:S(2)}) %copy-start.2) | copy-done | bytes 262168
  8.2 0.0 copy-start.3
  8.2 0.8 %copy-done.3 = f32[8,2,1024]{2,1,0:T(2,128)S(1)} copy-done((f32[8,2,1024]{2,1,0:T(2,128)S(1)}, f32[8,2,1024]{2,1,0:T(2,128)}, u32[]{:S(2)}) %copy-start.3) | copy-done | bytes 65560
  9.0 35.1 %shard_map.100 = bf16[192,1024]{1,0:T(8,128)(2,1)S(1)} custom-call(s32[16,128]{1,0:T(8,128)S(1)} %concatenate.3.meta_ref, bf16[1024,2048]{1,0:T(8,128)(2,1)S(1)} %bitcast.9, f32[8,2,1024]{2,1,0:T(2,128)S(1)} %copy-done.3, f32[32,2,1024]{2,1,0:T(2,128)S(1)} %copy-done.2, bf16[2,1024,64]{2,1,0:T(8,128)(2,1)S(1)} %copy.11.chan_ref, bf16[192,1024]{1,0:T(8,128)(2,1)S(1)} %copy-done.1), custom_call_target="tpu_custom_call" | custom-call | tf_op jit(solution)/shard_map/pallas_call | solution.py:238
  44.1 0.7 %copy.13 = bf16[192,1024]{1,0:T(8,128)(2,1)} copy(bf16[192,1024]{1,0:T(8,128)(2,1)S(1)} %shard_map.100) | data formatting | bytes 786432
  (1 shorter events, 0.0 us)
Async XLA Ops:
  4.0 2.2 %copy-start = (bf16[1,1024,2048]{2,1,0:T(8,128)(2,1)S(1)}, bf16[1,1024,2048]{2,1,0:T(8,128)(2,1)}, u32[]{:S(2)}) copy-start(bf16[1,1024,2048]{2,1,0:T(8,128)(2,1)} %param.10) | copy-start | bytes 12582916
  6.2 1.0 %copy-start.1 = (bf16[192,1024]{1,0:T(8,128)(2,1)S(1)}, bf16[192,1024]{1,0:T(8,128)(2,1)}, u32[]{:S(2)}) copy-start(bf16[192,1024]{1,0:T(8,128)(2,1)} %obs_hbm.1) | copy-start | bytes 1179652
  7.2 0.9 %copy-start.2 = (f32[32,2,1024]{2,1,0:T(2,128)S(1)}, f32[32,2,1024]{2,1,0:T(2,128)}, u32[]{:S(2)}) copy-start(f32[32,2,1024]{2,1,0:T(2,128)} %w_ref.1) | copy-start | bytes 786436
  8.2 0.8 %copy-start.3 = (f32[8,2,1024]{2,1,0:T(2,128)S(1)}, f32[8,2,1024]{2,1,0:T(2,128)}, u32[]{:S(2)}) copy-start(f32[8,2,1024]{2,1,0:T(2,128)} %a_ref.1) | copy-start | bytes 196612

commit v2 on v1

--- a/solution.py
+++ b/solution.py
@@ -38,21 +38,22 @@
 
 def kernel(
     n, cap, capp, ts, block,
-    meta_ref, grid_hbm, a_ref, w_ref, chan_ref, obs_hbm,
+    grid_hbm, powner_hbm, pcol_hbm, aper_hbm, windex_hbm, a_hbm, w_hbm, chan_hbm, towner_hbm, obs_hbm,
     out_ref,
-    grid, obs, rs, rq, acat, wcat, mat, tap, wt, sbuf, rbuf, wide, xbuf, sbuf2, rbuf2,
+    grid, powner, pcol, aper, windex, a_ref, w_ref, chan_ref, towner, obs, rs, rq, acat, wcat, mat, tap, wt, sbuf, rbuf, wide, xbuf, sbuf2, rbuf2,
     local_sem, send_sem, req_sem, pred_sem, time_sem,
 ):
     me = lax.axis_index("bl")
-    rows = meta_ref.shape[1]
+    rows = windex.shape[1]
     cells = grid.shape[1] // 2
     columns = grid.shape[0]
     span = cap * ts
 
-    load_grid = pltpu.make_async_copy(grid_hbm, grid, local_sem.at[0])
-    load_obs = pltpu.make_async_copy(obs_hbm, obs, local_sem.at[1])
-    load_grid.start()
-    load_obs.start()
+    pairs = [(powner_hbm, powner), (pcol_hbm, pcol), (aper_hbm, aper), (windex_hbm, windex), (towner_hbm, towner),
+             (a_hbm, a_ref), (w_hbm, w_ref), (chan_hbm, chan_ref), (grid_hbm, grid), (obs_hbm, obs)]
+    loads = [pltpu.make_async_copy(source, target, local_sem.at[k]) for k, (source, target) in enumerate(pairs)]
+    for load in loads:
+        load.start()
 
     barrier = pltpu.get_barrier_semaphore()
 
@@ -63,10 +64,16 @@
 
     lax.fori_loop(1, n, greet, 0)
 
-    meta = meta_ref[...]
-    p_owner, p_rank = owner_and_rank(meta[11:12], n)
-    t_owner, t_rank = owner_and_rank(meta[12:13], n)
-    data = jnp.concatenate([meta.astype(F32), jnp.zeros((LANES - 16, rows), F32)], axis=0).astype(BF16)
+    for load in loads[:5]:
+        load.wait()
+    p_owner, p_rank = owner_and_rank(powner[...], n)
+    t_owner, t_rank = owner_and_rank(towner[...], n)
+    column = pcol[...]
+    place = iota((8, rows), 0)
+    head = jnp.where(place == 0, jnp.right_shift(column, 5),
+                     jnp.where(place == 1, jnp.bitwise_and(column, 31), jnp.where(place == 2, aper[...], 0)))
+    data = jnp.concatenate([head.astype(F32), windex[...].astype(F32), jnp.zeros((LANES - 8 - ts, rows), F32)],
+                           axis=0).astype(BF16)
     wanted = dot_nt(one_hot_rows(p_owner * capp + p_rank, n * capp), data)
     rs[...] = wanted.reshape(n, capp, LANES)
 
@@ -103,6 +110,8 @@
     each(1, n, lambda i: request(i).start())
     rq[me] = rs[me]
 
+    for load in loads[5:8]:
+        load.wait()
     for part in range(2):
         at = pl.ds(part * cells, cells)
         for source, table in ((a_ref, acat), (w_ref, wcat)):
@@ -111,16 +120,13 @@
             high = value.astype(BF16)
             table[0:count, at] = high
             table[count:2 * count, at] = (value - high.astype(F32)).astype(BF16)
-    ch = chan_ref.shape[2]
-    left = (iota((ch, 2 * ch), 1) == iota((ch, 2 * ch), 0)).astype(F32).astype(BF16)
-    right = (iota((ch, 2 * ch), 1) == iota((ch, 2 * ch), 0) + ch).astype(F32).astype(BF16)
     real, imag = chan_ref[0], chan_ref[1]
-    mat[0:cells] = (dot(real, left) + dot(imag, right)).astype(BF16)
-    mat[cells:2 * cells] = (dot(real, right) - dot(imag, left)).astype(BF16)
+    mat[0:cells] = jnp.concatenate([real, imag], axis=0).T
+    mat[cells:2 * cells] = jnp.concatenate([-imag, real], axis=0).T
     move = dot_nt(one_hot_rows(t_owner * cap + t_rank, n * cap),
                   one_hot_rows(p_owner * cap + p_rank, n * cap)).astype(BF16)
 
-    load_grid.wait()
+    loads[8].wait()
     each(1, n, lambda i: arrival(rq, req_sem, i).wait())
 
     n_a = a_ref.shape[0]
@@ -155,7 +161,7 @@
         for j in range(block):
             req = spread(rq[lax.rem(me + c * block + j + 1, n), 0:cap, :])
             sample = iota((span, LANES), 0)
-            mine = iota((span, LANES), 1) == 3 + jnp.bitwise_and(sample, ts - 1)
+            mine = iota((span, LANES), 1) == 8 + jnp.bitwise_and(sample, ts - 1)
             plane = jnp.sum(jnp.where(mine, req, 0.0), axis=1, keepdims=True)
             lane = iota((span, 2 * n_w), 1)
             lane = jnp.where(lane >= n_w, lane - n_w, lane)
@@ -194,7 +200,7 @@
     sbuf2[...] = wide[...].astype(BF16).reshape(n, span, LANES)
     each(1, n, lambda i: timed(i).start())
     rbuf2[me] = sbuf2[me]
-    load_obs.wait()
+    loads[9].wait()
     each(1, n, lambda i: arrival(rbuf2, time_sem, i).wait())
 
     wide[...] = rbuf2[...].reshape(n * span, LANES).astype(F32)
@@ -230,18 +236,23 @@
     n_a, n_w = a_kernels.shape[0], w_kernels.shape[0]
     block = 4
     span = cap * ts
-    meta = jnp.concatenate(
-        [(patch_column >> 5)[None], (patch_column & 31)[None], aperture_index[None], w_index.T,
-         patch_owner.T, time_owner.T, jnp.zeros((3, rows), jnp.int32)], axis=0)
     vmem = pl.BlockSpec(memory_space=pltpu.VMEM)
-    hbm = pl.BlockSpec(memory_space=pl.ANY)
+    hbm = pl.BlockSpec(memory_space=pltpu.HBM)
     return pl.pallas_call(
         functools.partial(kernel, n, cap, capp, ts, block),
         out_shape=jax.ShapeDtypeStruct(observed.shape, BF16),
-        in_specs=[vmem, hbm, vmem, vmem, vmem, hbm],
+        in_specs=[hbm] * 10,
         out_specs=vmem,
         scratch_shapes=[
             pltpu.VMEM((columns, width), BF16),
+            pltpu.VMEM((1, rows), jnp.int32),
+            pltpu.VMEM((1, rows), jnp.int32),
+            pltpu.VMEM((1, rows), jnp.int32),
+            pltpu.VMEM((ts, rows), jnp.int32),
+            pltpu.VMEM(a_kernels.shape, F32),
+            pltpu.VMEM(w_kernels.shape, F32),
+            pltpu.VMEM((2, channel_response.shape[2], width // 2), BF16),
+            pltpu.VMEM((1, rows), jnp.int32),
             pltpu.VMEM(observed.shape, BF16),
             pltpu.VMEM((n, capp, LANES), F32),
             pltpu.VMEM((n, capp, LANES), F32),
@@ -256,15 +267,16 @@
             pltpu.VMEM((n * cap, ts * LANES), BF16),
             pltpu.VMEM((n, span, LANES), BF16),
             pltpu.VMEM((n, span, LANES), BF16),
-            pltpu.SemaphoreType.DMA((2,)),
+            pltpu.SemaphoreType.DMA((10,)),
             pltpu.SemaphoreType.DMA((3, n)),
             pltpu.SemaphoreType.DMA((n,)),
             pltpu.SemaphoreType.DMA((n,)),
             pltpu.SemaphoreType.DMA((n,)),
         ],
         compiler_params=pltpu.CompilerParams(
-            collective_id=0, has_side_effects=True, vmem_limit_bytes=48 * 1024 * 1024),
-    )(meta, grid.reshape(columns, width), a_kernels, w_kernels, channel_response, observed)
+            collective_id=0, has_side_effects=True, vmem_limit_bytes=64 * 1024 * 1024),
+    )(grid.reshape(columns, width), patch_owner.T, patch_column[None], aperture_index[None], w_index.T,
+      a_kernels, w_kernels, channel_response.transpose(0, 2, 1), time_owner.T, observed)
 
 
 def solution(mesh):

time: 45.2 us -> 37.5 us (0.83)
  the two profiles are of different devices: /device:TPU:27 before, /device:TPU:25 now
where the time goes in v2:
time: 37.5 us; the launch traced here: 37.4 us
  Pallas kernels  35.6 us (95%)
  local copies, waits for them, and re-layouts  1.77 us (5%)
    pallas_call x1, Pallas kernels, local(): pl.pallas_call(functools.partial(kernel, n, cap, capp, ts, block), out_sh...  35.6 us
    unnamed x1, local copies, waits for them, and re-layouts  1.77 us

profile of v2, /device:TPU:25, one launch (start us, length us, event | category | flops | bytes accessed | tf_op | source)
XLA Modules:
  0.0 37.4 jit_solution(6100567804942429902)
XLA Ops:
  0.0 35.6 %shard_map.100 = bf16[192,1024]{1,0:T(8,128)(2,1)} custom-call(bf16[1024,2048]{1,0:T(8,128)(2,1)} %bitcast.7, s32[1,128]{1,0:T(1,128)} %bitcast.10, s32[1,128]{1,0:T(1,128)} %bitcast.11, s32[1,128]{1,0:T(1,128)} %bitcast.12, s32[8,128]{1,0:T(8,128)} %bitcast.9, f32[8,2,1024]{2,1,0:T(2,128)} %a_hbm.1, f32[32,2,1024]{2,1,0:T(2,128)} %w_hbm.1, ...), custom_call_target="tpu_custom_call" | custom-call | tf_op jit(solution)/shard_map/pallas_call | solution.py:241
  35.6 1.8 %copy.12 = bf16[192,1024]{1,0:T(8,128)(2,1)} copy(bf16[192,1024]{1,0:T(8,128)(2,1)} %shard_map.100) | data formatting | bytes 786432

commit v3 on v2

v3 whole, which is shorter than its diff:
```python
import functools

import jax
import jax.numpy as jnp
from jax import lax
from jax.experimental import pallas as pl
from jax.experimental.pallas import tpu as pltpu
from jax.sharding import PartitionSpec as P

F32 = jnp.float32
BF16 = jnp.bfloat16
LANES = 128


def iota(shape, axis):
    return lax.broadcasted_iota(jnp.int32, shape, axis)


def dot(a, b):
    return jnp.dot(a, b, preferred_element_type=F32)


def dot_nt(a, b):
    return lax.dot_general(a, b, (((1,), (1,)), ((), ())), preferred_element_type=F32)


def owner_and_rank(owner, n):
    rows = owner.shape[1]
    hits = (iota((n, rows), 0) == owner).astype(F32)
    earlier = (iota((rows, rows), 0) < iota((rows, rows), 1)).astype(F32).astype(BF16)
    before = dot(hits.astype(BF16), earlier)
    return owner, jnp.sum(before * hits, axis=0, keepdims=True).astype(jnp.int32)


def one_hot_rows(slot, count):
    return (iota((count, slot.shape[1]), 0) == slot).astype(F32).astype(BF16)


def kernel(
    n, cap, capp, ts, block, halves,
    grid_hbm, powner_hbm, pcol_hbm, aper_hbm, windex_hbm, a_hbm, w_hbm, chan_hbm, towner_hbm, obs_hbm,
    out_ref,
    grid, powner, pcol, aper, windex, a_ref, w_ref, chan_ref, towner, obs, rs, rq, acat, wcat, mat, need, tap, wt, turn, sbuf, rbuf, wide, xbuf, sbuf2, rbuf2,
    local_sem, send_sem, req_sem, pred_sem, time_sem,
):
    me = lax.axis_index("bl")
    rows = windex.shape[1]
    cells = grid.shape[1] // 2
    columns = grid.shape[0]
    th = ts // halves
    span = cap * th
    total = n * cap

    def partner(k):
        there, bit = 0, 1
        while bit < n:
            there = there + bit * lax.rem(lax.div(me, bit) + lax.div(k, bit), 2)
            bit *= 2
        return there

    pairs = [(powner_hbm, powner), (pcol_hbm, pcol), (aper_hbm, aper), (windex_hbm, windex), (towner_hbm, towner),
             (a_hbm, a_ref), (w_hbm, w_ref), (chan_hbm, chan_ref), (grid_hbm, grid), (obs_hbm, obs)]
    loads = [pltpu.make_async_copy(source, target, local_sem.at[k]) for k, (source, target) in enumerate(pairs)]
    for load in loads:
        load.start()

    barrier = pltpu.get_barrier_semaphore()

    def greet(i, carry):
        pl.semaphore_signal(barrier, inc=1, device_id={"bl": lax.rem(me + i, n)},
                            device_id_type=pl.DeviceIdType.MESH)
        return carry

    lax.fori_loop(1, n, greet, 0)

    for load in loads[:5]:
        load.wait()
    p_owner, p_rank = owner_and_rank(powner[...], n)
    t_owner, t_rank = owner_and_rank(towner[...], n)
    column = pcol[...]
    place = iota((8, rows), 0)
    head = jnp.where(place == 0, jnp.right_shift(column, 5),
                     jnp.where(place == 1, jnp.bitwise_and(column, 31), jnp.where(place == 2, aper[...], 0)))
    data = jnp.concatenate([head.astype(F32), windex[...].astype(F32), jnp.zeros((LANES - 8 - ts, rows), F32)],
                           axis=0).astype(BF16)
    wanted = dot_nt(one_hot_rows(p_owner * capp + p_rank, n * capp), data)
    rs[...] = wanted.reshape(n, capp, LANES)

    pl.semaphore_wait(barrier, n - 1)

    def remote(source, target, sent_sem, there_sem, peer):
        return pltpu.make_async_remote_copy(
            src_ref=source, dst_ref=target, send_sem=sent_sem, recv_sem=there_sem,
            device_id={"bl": peer}, device_id_type=pl.DeviceIdType.MESH)

    def request(k):
        peer = partner(k)
        return remote(rs.at[peer], rq.at[me], send_sem.at[0, k], req_sem.at[me], peer)

    def predicted(h, k):
        return remote(sbuf.at[h, n - 1 - k], rbuf.at[h, me], send_sem.at[1 + h, k], pred_sem.at[h, me], partner(k))

    def timed(h, k):
        peer = partner(k)
        return remote(sbuf2.at[h, peer], rbuf2.at[h, me], send_sem.at[1 + halves + h, k], time_sem.at[h, me], peer)

    def arrival(buf, sem, k):
        sender = partner(k)
        return pltpu.make_async_copy(buf.at[sender], buf.at[sender], sem.at[sender])

    def each(act):
        def step(i, carry):
            act(n - 1 - i)
            return carry
        lax.fori_loop(0, n - 1, step, 0)

    each(lambda k: request(k).start())
    rq[me] = rs[me]

    for load in loads[5:8]:
        load.wait()
    for part in range(2):
        at = pl.ds(part * cells, cells)
        for source, table in ((a_ref, acat), (w_ref, wcat)):
            count = source.shape[0]
            value = source[:, part, :]
            high = value.astype(BF16)
            table[0:count, at] = high
            table[count:2 * count, at] = (value - high.astype(F32)).astype(BF16)
    real, imag = chan_ref[0], chan_ref[1]
    mat[0:cells] = jnp.concatenate([real, imag], axis=0).T
    mat[cells:2 * cells] = jnp.concatenate([-imag, real], axis=0).T
    move = dot_nt(one_hot_rows(t_owner * cap + t_rank, n * cap),
                  one_hot_rows(p_owner * cap + p_rank, n * cap)).astype(BF16)

    row = iota((total, 1), 0)
    turn_of = jnp.floor((row.astype(F32) + 0.5) / cap).astype(jnp.int32)
    source = jnp.bitwise_xor(n - 1 - turn_of, me) * capp + row - turn_of * cap
    compact = (iota((total, n * capp), 1) == source).astype(F32).astype(BF16)

    loads[8].wait()
    each(lambda k: arrival(rq, req_sem, k).wait())
    req = dot(compact, rq[...].reshape(n * capp, LANES).astype(BF16))
    need[...] = req

    n_a = a_ref.shape[0]
    wide_step = 256
    column = req[:, 0:1] * 32.0 + req[:, 1:2]
    pick = (iota((total, columns), 1).astype(F32) == column).astype(F32).astype(BF16)
    lane = iota((total, 2 * n_a), 1)
    lane = jnp.where(lane >= n_a, lane - n_a, lane)
    a_pick = (lane.astype(F32) == req[:, 2:3]).astype(F32).astype(BF16)
    for start in range(0, cells, wide_step):
        re, im = pl.ds(start, wide_step), pl.ds(cells + start, wide_step)
        p_re, p_im = dot(pick, grid[:, re]), dot(pick, grid[:, im])
        a_re, a_im = dot(a_pick, acat[:, re]), dot(a_pick, acat[:, im])
        tap[:, re] = p_re * a_re - p_im * a_im
        tap[:, im] = p_re * a_im + p_im * a_re

    n_w = w_ref.shape[0]
    lot = block * cap

    for h in range(halves):
        def predict(c, carry):
            at = pl.ds(pl.multiple_of(c * lot, 16), lot)
            plane = need[at, :]
            lane = iota((lot, 2 * n_w), 1)
            lane = jnp.where(lane >= n_w, lane - n_w, lane).astype(F32)
            w_pick = jnp.concatenate(
                [(lane == plane[:, 8 + h * th + t:9 + h * th + t]).astype(F32) for t in range(th)], axis=0).astype(BF16)
            for start in range(0, cells, wide_step):
                re, im = pl.ds(start, wide_step), pl.ds(cells + start, wide_step)
                s_re, s_im = dot(w_pick, wcat[:, re]), dot(w_pick, wcat[:, im])
                t_re, t_im = tap[at, re], tap[at, im]
                for t in range(th):
                    w_re, w_im = s_re[t * lot:(t + 1) * lot], s_im[t * lot:(t + 1) * lot]
                    wt[pl.ds(t * lot, lot), re] = (t_re * w_re - t_im * w_im).astype(BF16)
                    wt[pl.ds(t * lot, lot), im] = (t_re * w_im + t_im * w_re).astype(BF16)
            result = dot(wt[...], mat[...])
            for t in range(th):
                turn[pl.ds(t, lot, stride=th), :] = result[t * lot:(t + 1) * lot]
            sbuf[h, pl.ds(c * block, block)] = turn[...].astype(BF16).reshape(block, span, LANES)
            for j in range(block):
                k = n - 1 - (c * block + j)

                @pl.when(k > 0)
                def _():
                    predicted(h, k).start()
            return carry

        lax.fori_loop(0, n // block, predict, 0)
        rbuf[h, me] = sbuf[h, n - 1]

    for h in range(halves):
        each(lambda k: arrival(rbuf.at[h], pred_sem.at[h], k).wait())
        wide[...] = rbuf[h].reshape(n * span, LANES).astype(F32)
        for t in range(th):
            xbuf[:, pl.ds(t * LANES, LANES)] = wide[pl.ds(t, total, stride=th), :].astype(BF16)
        moved = dot(move, xbuf[...])
        for t in range(th):
            wide[pl.ds(t, total, stride=th), :] = moved[:, t * LANES:(t + 1) * LANES]
        sbuf2[h] = wide[...].astype(BF16).reshape(n, span, LANES)
        each(lambda k: timed(h, k).start())
        rbuf2[h, me] = sbuf2[h, me]
    loads[9].wait()
    for h in range(halves):
        each(lambda k: arrival(rbuf2.at[h], time_sem.at[h], k).wait())
        wide[...] = rbuf2[h].reshape(n * span, LANES).astype(F32)
        for t in range(th):
            at = pl.ds((h * th + t) * LANES, LANES)
            out_ref[:, at] = (obs[:, at].astype(F32) - wide[pl.ds(t, total, stride=th), :]).astype(BF16)

    def sent(k):
        request(k).wait_send()
        for h in range(halves):
            predicted(h, k).wait_send()
            timed(h, k).wait_send()

    each(sent)


def local(
    grid,
    patch_owner,
    patch_column,
    aperture_index,
    w_index,
    a_kernels,
    w_kernels,
    channel_response,
    time_owner,
    observed,
):
    n = lax.axis_size("bl")
    cap = observed.shape[0] // n
    capp = -(-cap // 8) * 8
    rows, ts = w_index.shape
    columns, width = grid.shape[1:]
    n_a, n_w = a_kernels.shape[0], w_kernels.shape[0]
    block = 4 if 4 * cap % 16 == 0 else 8
    halves = 2 if cap * ts // 2 % 16 == 0 else 1
    span = cap * ts // halves
    vmem = pl.BlockSpec(memory_space=pltpu.VMEM)
    hbm = pl.BlockSpec(memory_space=pltpu.HBM)
    return pl.pallas_call(
        functools.partial(kernel, n, cap, capp, ts, block, halves),
        out_shape=jax.ShapeDtypeStruct(observed.shape, BF16),
        in_specs=[hbm] * 10,
        out_specs=vmem,
        scratch_shapes=[
            pltpu.VMEM((columns, width), BF16),
            pltpu.VMEM((1, rows), jnp.int32),
            pltpu.VMEM((1, rows), jnp.int32),
            pltpu.VMEM((1, rows), jnp.int32),
            pltpu.VMEM((ts, rows), jnp.int32),
            pltpu.VMEM(a_kernels.shape, F32),
            pltpu.VMEM(w_kernels.shape, F32),
            pltpu.VMEM((2, channel_response.shape[2], width // 2), BF16),
            pltpu.VMEM((1, rows), jnp.int32),
            pltpu.VMEM(observed.shape, BF16),
            pltpu.VMEM((n, capp, LANES), F32),
            pltpu.VMEM((n, capp, LANES), F32),
            pltpu.VMEM((2 * n_a, width), BF16),
            pltpu.VMEM((2 * n_w, width), BF16),
            pltpu.VMEM((width, 2 * channel_response.shape[2]), BF16),
            pltpu.VMEM((n * cap, LANES), F32),
            pltpu.VMEM((n * cap, width), F32),
            pltpu.VMEM((block * span, width), BF16),
            pltpu.VMEM((block * span, LANES), F32),
            pltpu.VMEM((halves, n, span, LANES), BF16),
            pltpu.VMEM((halves, n, span, LANES), BF16),
            pltpu.VMEM((n * span, LANES), F32),
            pltpu.VMEM((n * cap, ts // halves * LANES), BF16),
            pltpu.VMEM((halves, n, span, LANES), BF16),
            pltpu.VMEM((halves, n, span, LANES), BF16),
            pltpu.SemaphoreType.DMA((10,)),
            pltpu.SemaphoreType.DMA((1 + 2 * halves, n)),
            pltpu.SemaphoreType.DMA((n,)),
            pltpu.SemaphoreType.DMA((halves, n)),
            pltpu.SemaphoreType.DMA((halves, n)),
        ],
        compiler_params=pltpu.CompilerParams(
            collective_id=0, has_side_effects=True, vmem_limit_bytes=64 * 1024 * 1024),
    )(grid.reshape(columns, width), patch_owner.T, patch_column[None], aperture_index[None], w_index.T,
      a_kernels, w_kernels, channel_response.transpose(0, 2, 1), time_owner.T, observed)


def solution(mesh):
    in_specs = (
        P(("groups", "bl"), None, None),
        P(("groups", "bl"), None),
        P(("groups", "bl")),
        P(("groups", "bl")),
        P(("groups", "bl"), None),
        P(),
        P(),
        P(None, None, "groups"),
        P(("groups", "bl"), None),
        P(("groups", "bl"), None),
    )
    out_specs = P(("groups", "bl"), None)
    return jax.shard_map(local, mesh=mesh, in_specs=in_specs, out_specs=out_specs, check_vma=False)
```

time: 37.5 us -> 36.3 us (0.968)
  the two profiles are of different devices: /device:TPU:25 before, /device:TPU:0 now
where the time goes in v3:
time: 36.3 us; the launch traced here: 36.1 us
  Pallas kernels  34.3 us (94%)
  local copies, waits for them, and re-layouts  1.77 us (5%)
    pallas_call x1, Pallas kernels, local(): pl.pallas_call(functools.partial(kernel, n, cap, capp, ts, block, halves)...  34.3 us
    unnamed x1, local copies, waits for them, and re-layouts  1.77 us

profile of v3, /device:TPU:0, one launch (start us, length us, event | category | flops | bytes accessed | tf_op | source)
XLA Modules:
  0.0 36.1 jit_solution(12434668086376125414)
XLA Ops:
  0.0 34.3 %shard_map.100 = bf16[192,1024]{1,0:T(8,128)(2,1)} custom-call(bf16[1024,2048]{1,0:T(8,128)(2,1)} %bitcast.7, s32[1,128]{1,0:T(1,128)} %bitcast.10, s32[1,128]{1,0:T(1,128)} %bitcast.11, s32[1,128]{1,0:T(1,128)} %bitcast.12, s32[8,128]{1,0:T(8,128)} %bitcast.9, f32[8,2,1024]{2,1,0:T(2,128)} %a_hbm.1, f32[32,2,1024]{2,1,0:T(2,128)} %w_hbm.1, ...), custom_call_target="tpu_custom_call" | custom-call | tf_op jit(solution)/shard_map/pallas_call | solution.py:245
  34.3 1.8 %copy.12 = bf16[192,1024]{1,0:T(8,128)(2,1)} copy(bf16[192,1024]{1,0:T(8,128)(2,1)} %shard_map.100) | data formatting | bytes 786432

commit v4 on v3

--- a/solution.py
+++ b/solution.py
@@ -51,11 +51,22 @@
     span = cap * th
     total = n * cap
 
-    def partner(k):
-        there, bit = 0, 1
-        while bit < n:
-            there = there + bit * lax.rem(lax.div(me, bit) + lax.div(k, bit), 2)
-            bit *= 2
+    group = min(n, 16)
+    flips, bit = [], 1
+    while bit < n:
+        flips.append(bit * (1 - 2 * lax.rem(lax.div(me, bit), 2)))
+        bit *= 2
+
+    def partner(high, low):
+        there = me
+        for place, flip in enumerate(flips):
+            if isinstance(high, int):
+                if (high + low) >> place & 1:
+                    there = there + flip
+            elif low >> place & 1:
+                there = there + flip
+            elif place >= 2:
+                there = there + flip * lax.rem(lax.div(high, 1 << place), 2)
         return there
 
     pairs = [(powner_hbm, powner), (pcol_hbm, pcol), (aper_hbm, aper), (windex_hbm, windex), (towner_hbm, towner),
@@ -71,7 +82,7 @@
                             device_id_type=pl.DeviceIdType.MESH)
         return carry
 
-    lax.fori_loop(1, n, greet, 0)
+    lax.fori_loop(1, n, greet, 0, unroll=n <= 16)
 
     for load in loads[:5]:
         load.wait()
@@ -84,7 +95,7 @@
     data = jnp.concatenate([head.astype(F32), windex[...].astype(F32), jnp.zeros((LANES - 8 - ts, rows), F32)],
                            axis=0).astype(BF16)
     wanted = dot_nt(one_hot_rows(p_owner * capp + p_rank, n * capp), data)
-    rs[...] = wanted.reshape(n, capp, LANES)
+    rs[...] = wanted.astype(BF16).reshape(n, capp, LANES)
 
     pl.semaphore_wait(barrier, n - 1)
 
@@ -93,28 +104,31 @@
             src_ref=source, dst_ref=target, send_sem=sent_sem, recv_sem=there_sem,
             device_id={"bl": peer}, device_id_type=pl.DeviceIdType.MESH)
 
-    def request(k):
-        peer = partner(k)
-        return remote(rs.at[peer], rq.at[me], send_sem.at[0, k], req_sem.at[me], peer)
-
-    def predicted(h, k):
-        return remote(sbuf.at[h, n - 1 - k], rbuf.at[h, me], send_sem.at[1 + h, k], pred_sem.at[h, me], partner(k))
-
-    def timed(h, k):
-        peer = partner(k)
-        return remote(sbuf2.at[h, peer], rbuf2.at[h, me], send_sem.at[1 + halves + h, k], time_sem.at[h, me], peer)
-
-    def arrival(buf, sem, k):
-        sender = partner(k)
-        return pltpu.make_async_copy(buf.at[sender], buf.at[sender], sem.at[sender])
+    def request(peer):
+        remote(rs.at[peer], rq.at[me], send_sem.at[0], req_sem, peer).start()
+
+    def predicted(h, index, peer):
+        remote(sbuf.at[h, index], rbuf.at[h, me], send_sem.at[1 + h], pred_sem.at[h], peer).start()
+
+    def timed(h, peer):
+        remote(sbuf2.at[h, peer], rbuf2.at[h, me], send_sem.at[1 + halves + h], time_sem.at[h], peer).start()
+
+    def all_of(buf, sem):
+        part = buf.at[pl.ds(0, n - 1)]
+        pltpu.make_async_copy(part, part, sem).wait()
 
     def each(act):
         def step(i, carry):
-            act(n - 1 - i)
+            high = n - group * (i + 1)
+            for low in reversed(range(group)):
+                act(partner(high, low))
             return carry
-        lax.fori_loop(0, n - 1, step, 0)
-
-    each(lambda k: request(k).start())
+        if n > group:
+            lax.fori_loop(0, n // group - 1, step, 0)
+        for low in reversed(range(1, group)):
+            act(partner(0, low))
+
+    each(request)
     rq[me] = rs[me]
 
     for load in loads[5:8]:
@@ -139,8 +153,8 @@
     compact = (iota((total, n * capp), 1) == source).astype(F32).astype(BF16)
 
     loads[8].wait()
-    each(lambda k: arrival(rq, req_sem, k).wait())
-    req = dot(compact, rq[...].reshape(n * capp, LANES).astype(BF16))
+    all_of(rq, req_sem)
+    req = dot(compact, rq[...].reshape(n * capp, LANES))
     need[...] = req
 
     n_a = a_ref.shape[0]
@@ -162,7 +176,7 @@
 
     for h in range(halves):
         def predict(c, carry):
-            at = pl.ds(pl.multiple_of(c * lot, 16), lot)
+            at = pl.ds(c * lot if isinstance(c, int) else pl.multiple_of(c * lot, 16), lot)
             plane = need[at, :]
             lane = iota((lot, 2 * n_w), 1)
             lane = jnp.where(lane >= n_w, lane - n_w, lane).astype(F32)
@@ -180,19 +194,28 @@
             for t in range(th):
                 turn[pl.ds(t, lot, stride=th), :] = result[t * lot:(t + 1) * lot]
             sbuf[h, pl.ds(c * block, block)] = turn[...].astype(BF16).reshape(block, span, LANES)
+            high = n - block * (c + 1)
             for j in range(block):
-                k = n - 1 - (c * block + j)
-
-                @pl.when(k > 0)
-                def _():
-                    predicted(h, k).start()
+                if isinstance(c, int) and high + block - 1 - j == 0:
+                    continue
+                peer = partner(high, block - 1 - j)
+                if isinstance(c, int) or j < block - 1:
+                    predicted(h, c * block + j, peer)
+                else:
+                    @pl.when(c < n // block - 1)
+                    def _():
+                        predicted(h, c * block + j, peer)
             return carry
 
-        lax.fori_loop(0, n // block, predict, 0)
+        if n // block <= 4:
+            for c in range(n // block):
+                predict(c, 0)
+        else:
+            lax.fori_loop(0, n // block, predict, 0)
         rbuf[h, me] = sbuf[h, n - 1]
 
     for h in range(halves):
-        each(lambda k: arrival(rbuf.at[h], pred_sem.at[h], k).wait())
+        all_of(rbuf.at[h], pred_sem.at[h])
         wide[...] = rbuf[h].reshape(n * span, LANES).astype(F32)
         for t in range(th):
             xbuf[:, pl.ds(t * LANES, LANES)] = wide[pl.ds(t, total, stride=th), :].astype(BF16)
@@ -200,23 +223,20 @@
         for t in range(th):
             wide[pl.ds(t, total, stride=th), :] = moved[:, t * LANES:(t + 1) * LANES]
         sbuf2[h] = wide[...].astype(BF16).reshape(n, span, LANES)
-        each(lambda k: timed(h, k).start())
+        each(functools.partial(timed, h))
         rbuf2[h, me] = sbuf2[h, me]
     loads[9].wait()
     for h in range(halves):
-        each(lambda k: arrival(rbuf2.at[h], time_sem.at[h], k).wait())
+        all_of(rbuf2.at[h], time_sem.at[h])
         wide[...] = rbuf2[h].reshape(n * span, LANES).astype(F32)
         for t in range(th):
             at = pl.ds((h * th + t) * LANES, LANES)
             out_ref[:, at] = (obs[:, at].astype(F32) - wide[pl.ds(t, total, stride=th), :]).astype(BF16)
 
-    def sent(k):
-        request(k).wait_send()
-        for h in range(halves):
-            predicted(h, k).wait_send()
-            timed(h, k).wait_send()
-
-    each(sent)
+    all_of(rs, send_sem.at[0])
+    for h in range(halves):
+        all_of(sbuf.at[h], send_sem.at[1 + h])
+        all_of(sbuf2.at[h], send_sem.at[1 + halves + h])
 
 
 def local(
@@ -233,7 +253,7 @@
 ):
     n = lax.axis_size("bl")
     cap = observed.shape[0] // n
-    capp = -(-cap // 8) * 8
+    capp = -(-cap // 16) * 16
     rows, ts = w_index.shape
     columns, width = grid.shape[1:]
     n_a, n_w = a_kernels.shape[0], w_kernels.shape[0]
@@ -258,8 +278,8 @@
             pltpu.VMEM((2, channel_response.shape[2], width // 2), BF16),
             pltpu.VMEM((1, rows), jnp.int32),
             pltpu.VMEM(observed.shape, BF16),
-            pltpu.VMEM((n, capp, LANES), F32),
-            pltpu.VMEM((n, capp, LANES), F32),
+            pltpu.VMEM((n, capp, LANES), BF16),
+            pltpu.VMEM((n, capp, LANES), BF16),
             pltpu.VMEM((2 * n_a, width), BF16),
             pltpu.VMEM((2 * n_w, width), BF16),
             pltpu.VMEM((width, 2 * channel_response.shape[2]), BF16),
@@ -274,10 +294,10 @@
             pltpu.VMEM((halves, n, span, LANES), BF16),
             pltpu.VMEM((halves, n, span, LANES), BF16),
             pltpu.SemaphoreType.DMA((10,)),
-            pltpu.SemaphoreType.DMA((1 + 2 * halves, n)),
-            pltpu.SemaphoreType.DMA((n,)),
-            pltpu.SemaphoreType.DMA((halves, n)),
-            pltpu.SemaphoreType.DMA((halves, n)),
+            pltpu.SemaphoreType.DMA((1 + 2 * halves,)),
+            pltpu.SemaphoreType.DMA,
+            pltpu.SemaphoreType.DMA((halves,)),
+            pltpu.SemaphoreType.DMA((halves,)),
         ],
         compiler_params=pltpu.CompilerParams(
             collective_id=0, has_side_effects=True, vmem_limit_bytes=64 * 1024 * 1024),

time: 36.3 us -> 33.8 us (0.931)
  Pallas kernels: 34.3 us -> 31.8 us
    pallas_call x1, Pallas kernels: 34.3 us -> 31.8 us  [local(): pl.pallas_call(functools.partial(kernel, n, cap, capp, ts, block, halves)...]
where the time goes in v4:
time: 33.8 us; the launch traced here: 33.6 us
  Pallas kernels  31.8 us (94%)
  local copies, waits for them, and re-layouts  1.77 us (5%)
    pallas_call x1, Pallas kernels, local(): pl.pallas_call(functools.partial(kernel, n, cap, capp, ts, block, halves)...  31.8 us
    unnamed x1, local copies, waits for them, and re-layouts  1.77 us

profile of v4, /device:TPU:0, one launch (start us, length us, event | category | flops | bytes accessed | tf_op | source)
XLA Modules:
  0.0 33.6 jit_solution(11620092282515024332)
XLA Ops:
  0.0 31.8 %shard_map.100 = bf16[192,1024]{1,0:T(8,128)(2,1)} custom-call(bf16[1024,2048]{1,0:T(8,128)(2,1)} %bitcast.7, s32[1,128]{1,0:T(1,128)} %bitcast.10, s32[1,128]{1,0:T(1,128)} %bitcast.11, s32[1,128]{1,0:T(1,128)} %bitcast.12, s32[8,128]{1,0:T(8,128)} %bitcast.9, f32[8,2,1024]{2,1,0:T(2,128)} %a_hbm.1, f32[32,2,1024]{2,1,0:T(2,128)} %w_hbm.1, ...), custom_call_target="tpu_custom_call" | custom-call | tf_op jit(solution)/shard_map/pallas_call | solution.py:265
  31.8 1.8 %copy.12 = bf16[192,1024]{1,0:T(8,128)(2,1)} copy(bf16[192,1024]{1,0:T(8,128)(2,1)} %shard_map.100) | data formatting | bytes 786432

commit v5 on v4

--- a/solution.py
+++ b/solution.py
@@ -69,20 +69,20 @@
                 there = there + flip * lax.rem(lax.div(high, 1 << place), 2)
         return there
 
+    barrier = pltpu.get_barrier_semaphore()
+
+    def greet(i, carry):
+        pl.semaphore_signal(barrier, inc=1, device_id={"bl": lax.rem(me + i, n)},
+                            device_id_type=pl.DeviceIdType.MESH)
+        return carry
+
+    lax.fori_loop(1, n, greet, 0, unroll=n <= 16)
+
     pairs = [(powner_hbm, powner), (pcol_hbm, pcol), (aper_hbm, aper), (windex_hbm, windex), (towner_hbm, towner),
              (a_hbm, a_ref), (w_hbm, w_ref), (chan_hbm, chan_ref), (grid_hbm, grid), (obs_hbm, obs)]
     loads = [pltpu.make_async_copy(source, target, local_sem.at[k]) for k, (source, target) in enumerate(pairs)]
     for load in loads:
         load.start()
-
-    barrier = pltpu.get_barrier_semaphore()
-
-    def greet(i, carry):
-        pl.semaphore_signal(barrier, inc=1, device_id={"bl": lax.rem(me + i, n)},
-                            device_id_type=pl.DeviceIdType.MESH)
-        return carry
-
-    lax.fori_loop(1, n, greet, 0, unroll=n <= 16)
 
     for load in loads[:5]:
         load.wait()
@@ -159,20 +159,25 @@
 
     n_a = a_ref.shape[0]
     wide_step = 256
-    column = req[:, 0:1] * 32.0 + req[:, 1:2]
-    pick = (iota((total, columns), 1).astype(F32) == column).astype(F32).astype(BF16)
-    lane = iota((total, 2 * n_a), 1)
-    lane = jnp.where(lane >= n_a, lane - n_a, lane)
-    a_pick = (lane.astype(F32) == req[:, 2:3]).astype(F32).astype(BF16)
-    for start in range(0, cells, wide_step):
-        re, im = pl.ds(start, wide_step), pl.ds(cells + start, wide_step)
-        p_re, p_im = dot(pick, grid[:, re]), dot(pick, grid[:, im])
-        a_re, a_im = dot(a_pick, acat[:, re]), dot(a_pick, acat[:, im])
-        tap[:, re] = p_re * a_re - p_im * a_im
-        tap[:, im] = p_re * a_im + p_im * a_re
+
+    def taper(first, count):
+        at = pl.ds(first, count)
+        mine = need[at, :]
+        column = mine[:, 0:1] * 32.0 + mine[:, 1:2]
+        pick = (iota((count, columns), 1).astype(F32) == column).astype(F32).astype(BF16)
+        lane = iota((count, 2 * n_a), 1)
+        lane = jnp.where(lane >= n_a, lane - n_a, lane)
+        a_pick = (lane.astype(F32) == mine[:, 2:3]).astype(F32).astype(BF16)
+        for start in range(0, cells, wide_step):
+            re, im = pl.ds(start, wide_step), pl.ds(cells + start, wide_step)
+            p_re, p_im = dot(pick, grid[:, re]), dot(pick, grid[:, im])
+            a_re, a_im = dot(a_pick, acat[:, re]), dot(a_pick, acat[:, im])
+            tap[at, re] = p_re * a_re - p_im * a_im
+            tap[at, im] = p_re * a_im + p_im * a_re
 
     n_w = w_ref.shape[0]
     lot = block * cap
+    run = 2
 
     for h in range(halves):
         def predict(c, carry):
@@ -209,8 +214,12 @@
 
         if n // block <= 4:
             for c in range(n // block):
+                if h == 0 and c % run == 0:
+                    taper(c * lot, run * lot)
                 predict(c, 0)
         else:
+            if h == 0:
+                taper(0, total)
             lax.fori_loop(0, n // block, predict, 0)
         rbuf[h, me] = sbuf[h, n - 1]
 

time: 33.8 us -> 33.4 us (0.988)
  no operation moved by 1% of the time
where the time goes in v5:
time: 33.4 us; the launch traced here: 33.3 us
  Pallas kernels  31.5 us (94%)
  local copies, waits for them, and re-layouts  1.77 us (5%)
    pallas_call x1, Pallas kernels, local(): pl.pallas_call(functools.partial(kernel, n, cap, capp, ts, block, halves)...  31.5 us
    unnamed x1, local copies, waits for them, and re-layouts  1.77 us

profile of v5, /device:TPU:0, one launch (start us, length us, event | category | flops | bytes accessed | tf_op | source)
XLA Modules:
  0.0 33.3 jit_solution(10831504478156192558)
XLA Ops:
  0.0 31.5 %shard_map.100 = bf16[192,1024]{1,0:T(8,128)(2,1)} custom-call(bf16[1024,2048]{1,0:T(8,128)(2,1)} %bitcast.7, s32[1,128]{1,0:T(1,128)} %bitcast.10, s32[1,128]{1,0:T(1,128)} %bitcast.11, s32[1,128]{1,0:T(1,128)} %bitcast.12, s32[8,128]{1,0:T(8,128)} %bitcast.9, f32[8,2,1024]{2,1,0:T(2,128)} %a_hbm.1, f32[32,2,1024]{2,1,0:T(2,128)} %w_hbm.1, ...), custom_call_target="tpu_custom_call" | custom-call | tf_op jit(solution)/shard_map/pallas_call | solution.py:274
  31.5 1.8 %copy.12 = bf16[192,1024]{1,0:T(8,128)(2,1)} copy(bf16[192,1024]{1,0:T(8,128)(2,1)} %shard_map.100) | data formatting | bytes 786432
